TPU v7x, 32 devices: a whole 2x2x4 slice. The times are simulated.
32 devices in a mesh: group: 2 (over x), req: 8 (over z, y), chan: 2 (over core).
Axes of the slice: x: 2, y: 2, z: 4, core: 2. Of those that a mesh axis runs over, the one named last changes fastest.
Arguments:
- value_stream: bfloat16 [32, 32, 8192], P(('group', 'req'), None, 'chan'), parts along dimension 0, may hold values from -6 to 6
- gate_stream: bfloat16 [32, 32, 8192], P(('group', 'req'), None, 'chan'), parts along dimension 0, may hold values from -6 to 6
- key_query_stream: bfloat16 [32, 32, 4, 512], P(('group', 'req'), None, 'chan'), parts along dimension 0, may hold values from -6 to 6
- step_stream: bfloat16 [32, 32, 128], P(('group', 'req'), None, 'chan'), parts along dimension 0, may hold values from -6 to 6
- parents: int32 [32, 32], P(('group', 'req')), parts along dimension 0, may hold values from -1 to 30, as said below
- tree_sizes: int32 [32], P(('group', 'req')), parts along dimension 0, may hold values from 1 to 32, as said below
- slot_index: int32 [32], P(('group', 'req')), parts along dimension 0, may hold values from 0 to 15, as said below
- value_cache: bfloat16 [32, 3, 8192], P(('group', 'req'), None, 'chan'), parts along dimension 0, may hold values from -6 to 6
- key_query_cache: bfloat16 [32, 3, 4, 512], P(('group', 'req'), None, 'chan'), parts along dimension 0, may hold values from -6 to 6
- value_conv: bfloat16 [4, 8192], P(None, 'chan'), may hold values from -3 to 3
- key_query_conv: bfloat16 [4, 4, 512], P(None, 'chan'), may hold values from -3 to 3
- step_bias: float32 [128], P('chan'), may hold values from -4 to -1
- log_rate: float32 [128], P('chan'), may hold values from -1 to 2
- skip_gain: float32 [128], P('chan'), may hold values from 0.5 to 1.5
- norm_gain: bfloat16 [8192], P('chan'), may hold values from 0.5 to 1.5
- cached_state: float32 [32, 128, 64, 256], P(('group', 'req'), 'chan'), parts along dimension 0, may hold values from -2 to 2
- out_weight: bfloat16 [8192, 8192], P('chan', 'req'), may hold values from -0.0625 to 0.0625
Outputs:
- layer_out: bfloat16 [32, 32, 8192], P(('group', 'req'), 'chan'), parts along dimension 0
- final_state: float32 [32, 128, 64, 256], P(('group', 'req'), 'chan'), parts along dimension 0
There are 2 independent parts, one for each index of `group`. A program takes and returns all parts, laid end to end along the dimension named above; an argument that names none is the same for every part. Nothing has to cross between parts.
Inputs may be any that keep to these rules, and one draw needn't show every extreme that they name: parents[r, 0] = -1 for the root; for n >= 1, parents[r, n] lies in 0 to n - 1. `tree_sizes`: each size is at least 1; nodes at indices from the size on are padding. The 2 trees of one aligned block of 2 requests hold together at most 48 live nodes, and some block holds exactly 48. `slot_index`: A permutation of the requests that maps each aligned block of 2 requests onto itself.
All inputs are finite; a program needn't handle non-finite values.
Results may differ from a plain program's by a relative error of at most 0.0049.
Values may be sent and summed in bfloat16 or wider, within the bound.
A program may use at most 128 MiB of HBM per device.

v0:
```python
import jax
import jax.numpy as jnp
from jax import lax
from jax.sharding import PartitionSpec as P

highest = lax.Precision.HIGHEST
norm_epsilon = 1e-05


def ancestry(parents):
    node_count = parents.shape[-1]
    node_ids = jnp.arange(node_count, dtype=jnp.int32)
    step_one = (parents[:, :, None] == node_ids[None, None, :]).astype(jnp.float32)
    identity_mat = jnp.broadcast_to(jnp.eye(node_count, dtype=jnp.float32), step_one.shape)
    ancestors = identity_mat + step_one
    jump_power = step_one
    reach_span = 2
    while reach_span < node_count:
        jump_power = jnp.einsum("rnj,rjk->rnk", jump_power, jump_power, precision=highest)
        ancestors = jnp.einsum(
            "rnj,rjk->rnk", ancestors, identity_mat + jump_power, precision=highest
        )
        reach_span = reach_span * 2
    second_power = jnp.einsum("rnj,rjk->rnk", step_one, step_one, precision=highest)
    third_power = jnp.einsum("rnj,rjk->rnk", second_power, step_one, precision=highest)
    return (
        ancestors,
        (
            step_one.astype(jnp.bfloat16),
            second_power.astype(jnp.bfloat16),
            third_power.astype(jnp.bfloat16),
        ),
    )


def tree_conv(values, cache, weight, shifts, node_depth):
    conv_sum = weight[3].astype(jnp.float32) * values.astype(jnp.float32)
    cache_rows = jnp.arange(3, dtype=jnp.int32)
    for lookback in (1, 2, 3):
        earlier = jnp.einsum(
            "rnj,rjc->rnc", shifts[lookback - 1], values, preferred_element_type=jnp.float32
        )
        cache_slot = 3 - lookback + node_depth
        chooser = (
            (node_depth < lookback)[:, :, None]
            & (cache_slot[:, :, None] == cache_rows[None, None, :])
        ).astype(jnp.bfloat16)
        earlier = earlier + jnp.einsum(
            "rnq,rqc->rnc", chooser, cache, preferred_element_type=jnp.float32
        )
        conv_sum = conv_sum + weight[3 - lookback].astype(jnp.float32) * earlier
    return jax.nn.silu(conv_sum)


def tree_layer(
    value_rows,
    gate_rows,
    kq_rows,
    step_rows,
    parents,
    tree_sizes,
    value_cache,
    key_query_cache,
    value_conv,
    key_query_conv,
    step_bias,
    log_rate,
    skip_gain,
    norm_gain,
    cached_state,
):
    req_count, node_count, channels = value_rows.shape
    groups = kq_rows.shape[2]
    state_width = kq_rows.shape[3] // 2
    head_count = step_rows.shape[2]
    per_group = head_count // groups
    head_dim = channels // head_count
    ancestors, shifts = ancestry(parents)
    node_depth = (jnp.sum(ancestors, axis=-1) - 1.0).astype(jnp.int32)
    conv_values = tree_conv(value_rows, value_cache, value_conv, shifts, node_depth)
    conv_kq = tree_conv(
        kq_rows.reshape(req_count, node_count, -1),
        key_query_cache.reshape(req_count, 3, -1),
        key_query_conv.reshape(key_query_conv.shape[0], -1),
        shifts,
        node_depth,
    )
    conv_kq = conv_kq.reshape(req_count, node_count, groups, 2 * state_width)
    key_rows = conv_kq[..., :state_width]
    queries = conv_kq[..., state_width:]
    step_size = jax.nn.softplus(step_rows.astype(jnp.float32) + step_bias)
    log_level = jnp.einsum(
        "rnj,rjh->rnh", ancestors, step_size * -jnp.exp(log_rate), precision=highest
    )
    level_gap = log_level[:, :, None, :] - log_level[:, None, :, :]
    path_decay = jnp.exp(jnp.where(ancestors[:, :, :, None] > 0.5, level_gap, -jnp.inf))
    affinity = jnp.einsum("rngs,rjgs->rnjg", queries, key_rows, precision=highest)
    affinity = jnp.repeat(affinity, per_group, axis=3)
    weights = affinity * path_decay * step_size[:, None, :, :]
    values = conv_values.reshape(req_count, node_count, head_count, head_dim)
    inner_out = jnp.einsum("rnjh,rjhp->rnhp", weights, values, precision=highest)
    state_grouped = cached_state.reshape(req_count, groups, per_group, head_dim, state_width)
    carried = jnp.einsum("rngs,rgkps->rngkp", queries, state_grouped, precision=highest)
    carried = carried.reshape(req_count, node_count, head_count, head_dim)
    result = (
        inner_out
        + carried * jnp.exp(log_level)[..., None]
        + skip_gain[None, None, :, None] * values
    )
    last_pick = (jnp.arange(node_count)[None, :] == (tree_sizes - 1)[:, None]).astype(jnp.float32)
    last_decay = jnp.einsum("rn,rnjh->rjh", last_pick, path_decay, precision=highest)
    last_level = jnp.einsum("rn,rnh->rh", last_pick, log_level, precision=highest)
    scaled = (values * (last_decay * step_size)[..., None]).reshape(
        req_count, node_count, groups, per_group, head_dim
    )
    update = jnp.einsum("rjgkp,rjgs->rgkps", scaled, key_rows, precision=highest).reshape(
        cached_state.shape
    )
    final_state = jnp.exp(last_level)[:, :, None, None] * cached_state + update
    gated = result.reshape(req_count, node_count, channels) * jax.nn.silu(
        gate_rows.astype(jnp.float32)
    )
    blocks = gated.reshape(req_count, node_count, groups, -1)
    inverse_rms = lax.rsqrt(jnp.mean(blocks * blocks, axis=-1, keepdims=True) + norm_epsilon)
    normed = (blocks * inverse_rms).reshape(req_count, node_count, channels) * norm_gain.astype(
        jnp.float32
    )
    live_mask = jnp.arange(node_count)[None, :] < tree_sizes[:, None]
    hidden = jnp.where(live_mask[:, :, None], normed, 0.0).astype(jnp.bfloat16)
    return (hidden, final_state)


def local(
    value_stream,
    gate_stream,
    key_query_stream,
    step_stream,
    parents,
    tree_sizes,
    slot_index,
    value_cache,
    key_query_cache,
    value_conv,
    key_query_conv,
    step_bias,
    log_rate,
    skip_gain,
    norm_gain,
    cached_state,
    out_weight,
):
    req_count, node_count = parents.shape
    slot_order = slot_index % req_count
    hidden, final_state = tree_layer(
        jnp.take(value_stream, slot_order, axis=0),
        jnp.take(gate_stream, slot_order, axis=0),
        jnp.take(key_query_stream, slot_order, axis=0),
        jnp.take(step_stream, slot_order, axis=0),
        parents,
        tree_sizes,
        value_cache,
        key_query_cache,
        value_conv,
        key_query_conv,
        step_bias,
        log_rate,
        skip_gain,
        norm_gain,
        cached_state,
    )
    flat_rows = hidden.reshape(req_count * node_count, -1)
    req_devices = lax.axis_size("req")
    partial_terms = jnp.dot(
        lax.all_gather(flat_rows, "req", axis=0, tiled=True),
        out_weight,
        preferred_element_type=jnp.float32,
    )
    column_block = partial_terms.shape[-1]
    split_terms = partial_terms.reshape(req_devices, req_count, node_count, column_block)
    scatter_dim = split_terms.ndim - 2
    shares = lax.psum_scatter(
        split_terms, "chan", scatter_dimension=scatter_dim, tiled=True
    ).astype(jnp.bfloat16)
    mine = lax.all_to_all(shares, "req", split_axis=0, concat_axis=shares.ndim - 1, tiled=True)[0]
    return (mine, final_state)


def solution(mesh):
    return jax.shard_map(
        local,
        mesh=mesh,
        in_specs=(
            P(("group", "req"), None, "chan"),
            P(("group", "req"), None, "chan"),
            P(("group", "req"), None, "chan", None),
            P(("group", "req"), None, "chan"),
            P(("group", "req"), None),
            P(("group", "req")),
            P(("group", "req")),
            P(("group", "req"), None, "chan"),
            P(("group", "req"), None, "chan", None),
            P(None, "chan"),
            P(None, "chan", None),
            P("chan"),
            P("chan"),
            P("chan"),
            P("chan"),
            P(("group", "req"), "chan", None, None),
            P("chan", "req"),
        ),
        out_specs=(P(("group", "req"), "chan", None), P(("group", "req"), "chan", None, None)),
        check_vma=False,
    )
```

profile of v0, /device:TPU:0, one launch (start us, length us, event | category | flops | bytes accessed | tf_op | source)
XLA Modules:
  0.0 199.8 jit_solution(3499961693872958279)
XLA Ops:
  7.3 0.7 broadcast_add_fusion.2
  8.0 1.3 iota_compare_fusion.9
  9.3 0.9 fusion.58
  10.2 0.9 convolution_convert_fusion
  11.5 0.9 fusion.50
  12.4 0.2 convolution_add_fusion.6
  12.6 0.2 fusion.55
  12.7 0.2 fusion.53
  12.9 0.3 fusion.105
  13.2 0.7 compare_and_fusion
  13.9 1.7 gather_fusion
  15.7 1.6 fusion.59
  17.4 0.2 fusion.70
  17.6 0.6 fusion.98
  18.2 0.6 gather_fusion.1
  18.8 0.6 convert_element_type.183
  19.4 0.6 copy.73
  20.0 0.6 copy.74
  20.7 0.3 fusion.106
  21.1 0.7 copy.55
  21.8 1.3 fusion.11
  23.3 0.7 copy.53
  24.0 0.7 slice_convert_fusion.3
  24.7 0.2 fusion.102
  25.0 0.4 fusion.44
  25.4 0.4 fusion.46
  25.8 0.2 fusion.18
  26.0 0.2 fusion.17
  26.3 1.4 fusion.48
  27.6 0.9 divide_multiply_fusion.1
  28.6 0.2 reshape.198
  28.9 0.2 convolution_bitcast_fusion
  29.1 0.7 copy.48
  29.8 0.7 gather_fusion.2
  30.5 1.7 gather_fusion.3
  32.3 14.6 %fusion.38 = f32[2,2,32,32,64]{4,2,3,1,0:T(8,128)} fusion(f32[2,2,32,64,256]{4,3,2,1,0:T(8,128)} %bitcast.77, f32[2,32,2,256]{3,2,1,0:T(2,128)S(1)} %get-tuple-element.6), kind=kOutput, calls=%fused_computation.57 | convolution fusion | flops 805306368 | bytes 9568256 | tf_op jit(solution)/shard_map/rngs,rgkps->rngkp/dot_general | solution.py:103
  47.0 0.4 fusion.5
  47.4 0.3 copy-done.15
  47.7 0.3 fusion.4
  48.1 0.2 copy-done.3
  48.2 1.6 divide_multiply_fusion
  49.9 2.2 %reshape.196 = f32[2,32,64,64]{3,2,1,0:T(8,128)S(1)} reshape(f32[2,32,4096]{2,1,0:T(8,128)} %divide_multiply_fusion) | data formatting | bytes 2097152 | tf_op jit(solution)/shard_map/reshape | solution.py:100
  52.1 0.3 broadcast_in_dim.68
  52.4 1.3 copy-done.2
  53.7 5.0 %fusion.6 = f32[2,32,64,64]{3,1,2,0:T(8,128)S(1)} fusion(f32[2,32,64,64]{3,1,2,0:T(8,128)S(1)} %bitcast.80, f32[2,32,64,64]{3,2,1,0:T(8,128)S(1)} %reshape.196, f32[2,32,32,64]{2,1,3,0:T(8,128)S(1)} %bitcast.79, f32[64]{0:T(128)S(1)} %copy-done.37, f32[2,32,64]{1,2,0:T(8,128)S(1)} %copy-done.5, f32[2,32,64]{1,2,0:T(8,128)S(1)} %copy-done.6, ...), kind=kOutput, calls=%fused_computation.15 | convolution fusion | flops 102236160 | bytes 3721472 | tf_op jit(solution)/shard_map/rnjh,rjhp->rnhp/dot_general | solution.py:101
  58.7 2.5 %copy.57 = f32[2,32,64,64]{3,2,1,0:T(8,128)} copy(f32[2,32,64,64]{3,1,2,0:T(8,128)S(1)} %fusion.6) | data formatting | bytes 2097152 | tf_op jit(solution)/shard_map/add | solution.py:106
  61.2 2.1 %reshape.202 = f32[2,32,4096]{2,1,0:T(8,128)S(1)} reshape(f32[2,32,64,64]{3,2,1,0:T(8,128)} %copy.57) | data formatting | bytes 2097152 | tf_op jit(solution)/shard_map/reshape | solution.py:120
  63.4 1.4 fusion.103
  64.7 2.1 %mul.190 = f32[2,32,2,2048]{3,2,1,0:T(2,128)S(1)} reshape(f32[2,32,4096]{2,1,0:T(8,128)} %fusion.103) | data formatting | bytes 2097152 | tf_op jit(solution)/shard_map/mul | solution.py:124
  66.9 0.4 reduce_sum.19
  67.2 1.3 mul.191
  68.5 2.1 %mul.192 = f32[2,32,4096]{2,1,0:T(8,128)S(1)} reshape(f32[2,32,2,2048]{3,2,1,0:T(2,128)} %mul.191) | data formatting | bytes 2097152 | tf_op jit(solution)/shard_map/mul | solution.py:125
  70.7 1.3 select_convert_fusion
  72.0 0.3 reduce-scatter.2.cloned.1.call-start
  72.3 76.0 %all-gather.2.cloned.1.call-done = bf16[512,4096]{1,0:T(8,128)(2,1)} async-done(((bf16[64,4096]{1,0:T(8,128)(2,1)}), bf16[512,4096]{1,0:T(8,128)(2,1)}) %all-gather.2.cloned.1.call-update) | async-done | bytes 4194320 | tf_op jit(solution)/shard_map/all_gather | solution.py:174
  148.2 10.5 %fusion.109 = f32[512,1024]{1,0:T(8,128)} fusion(bf16[512,4096]{1,0:T(8,128)(2,1)} %all-gather.2.cloned.1.call-done, bf16[4096,1024]{1,0:T(8,128)(2,1)} %param.35), kind=kOutput, calls=%fused_computation.158 | convolution fusion | flops 4294967296 | bytes 14680064 | tf_op jit(solution)/shard_map/dot_general | solution.py:173
  158.8 2.0 %reshape.205 = f32[2,32,2,32,64]{4,3,2,1,0:T(8,128)S(1)} reshape(f32[2,32,4096]{2,1,0:T(8,128)} %divide_multiply_fusion) | data formatting | bytes 2097152 | tf_op jit(solution)/shard_map/reshape | solution.py:100
  160.9 11.1 %fusion.7 = f32[2,2,32,64,256]{4,3,2,1,0:T(8,128)} fusion(f32[2,32,2,32,64]{4,3,2,1,0:T(8,128)S(1)} %reshape.205, f32[2,32,2,32]{1,3,2,0:T(8,128)S(1)} %bitcast.84, f32[2,32,2,256]{3,2,1,0:T(2,128)S(1)} %get-tuple-element.5), kind=kOutput, calls=%fused_computation.17 | convolution fusion | flops 805568512 | bytes 9584640 | tf_op jit(solution)/shard_map/rjgkp,rjgs->rgkps/dot_general | solution.py:116
  172.0 2.1 %convert_element_type.185 = bf16[8,2,16,1024]{3,2,1,0:T(8,128)(2,1)} convert(f32[8,2,16,1024]{3,2,1,0:T(8,128)} %reduce-scatter.2.cloned.1.call-done) | non-fusion elementwise | flops 262144 | bytes 1572864 | tf_op jit(solution)/shard_map/convert_element_type | solution.py:183
  174.1 3.5 %all-to-all-start = ((bf16[8,2,16,1024]{3,2,1,0:T(8,128)(2,1)}), bf16[8,2,16,1024]{3,2,1,0:T(8,128)(2,1)S(1)}, u32[]{:S(2)}, u32[]{:S(2)}) async-start(bf16[8,2,16,1024]{3,2,1,0:T(8,128)(2,1)} %convert_element_type.185), calls=%async_computation.1 | async-start | bytes 1048576 | tf_op jit(solution)/shard_map/all_to_all | solution.py:184
  177.8 10.1 %multiply_add_fusion = f32[2,64,64,256]{3,2,1,0:T(8,128)} fusion(f32[2,64,64,256]{3,2,1,0:T(8,128)} %bitcast.78, f32[2,64,64,256]{3,2,1,0:T(8,128)} %param.34, f32[2,64]{1,0:T(2,128)S(1)} %exp.38), kind=kLoop, calls=%fused_computation.4 | loop fusion | flops 4194304 | bytes 25166336 | tf_op jit(solution)/shard_map/add | solution.py:119
  187.9 3.8 %all-to-all-done = bf16[8,2,16,1024]{3,2,1,0:T(8,128)(2,1)S(1)} async-done(((bf16[8,2,16,1024]{3,2,1,0:T(8,128)(2,1)}), bf16[8,2,16,1024]{3,2,1,0:T(8,128)(2,1)S(1)}, u32[]{:S(2)}, u32[]{:S(2)}) %all-to-all-start) | async-done | bytes 524320 | tf_op jit(solution)/shard_map/all_to_all | solution.py:184
  191.7 0.3 copy.58
  192.0 1.0 squeeze.2
  (104 shorter events, 1.3 us)
Async XLA Ops:
  7.2 22.7 %copy-start = (bf16[2,32,4096]{2,1,0:T(8,128)(2,1)S(1)}, bf16[2,32,4096]{2,1,0:T(8,128)(2,1)}, u32[]{:S(2)}) copy-start(bf16[2,32,4096]{2,1,0:T(8,128)(2,1)} %param.19) | copy-start | bytes 1572868
  7.2 10.4 %copy-start.39 = (f32[64]{0:T(128)S(1)}, f32[64]{0:T(128)}, u32[]{:S(2)}) copy-start(f32[64]{0:T(128)} %param.31) | copy-start | bytes 772
  7.2 11.0 %copy-start.26 = (bf16[2,3,2,512]{3,2,1,0:T(2,128)(2,1)S(1)}, bf16[2,3,2,512]{3,2,1,0:T(2,128)(2,1)}, u32[]{:S(2)}) copy-start(bf16[2,3,2,512]{3,2,1,0:T(2,128)(2,1)} %param.27) | copy-start | bytes 36868
  7.2 11.0 %copy-start.23 = (bf16[2,32,64]{2,1,0:T(8,128)(2,1)S(1)}, bf16[2,32,64]{2,1,0:T(8,128)(2,1)}, u32[]{:S(2)}) copy-start(bf16[2,32,64]{2,1,0:T(8,128)(2,1)} %param.22) | copy-start | bytes 24580
  7.2 11.6 %copy-start.28 = (bf16[4096]{0:T(1024)(128)(2,1)S(1)}, bf16[4096]{0:T(1024)(128)(2,1)}, u32[]{:S(2)}) copy-start(bf16[4096]{0:T(1024)(128)(2,1)} %param.33) | copy-start | bytes 24580
  7.2 12.2 %copy-start.29 = (bf16[4,2,512]{2,1,0:T(2,128)(2,1)S(1)}, bf16[4,2,512]{2,1,0:T(2,128)(2,1)}, u32[]{:S(2)}) copy-start(bf16[4,2,512]{2,1,0:T(2,128)(2,1)} %param.29) | copy-start | bytes 24580
  7.2 13.5 %copy-start.36 = (f32[64]{0:T(128)S(1)}, f32[64]{0:T(128)}, u32[]{:S(2)}) copy-start(f32[64]{0:T(128)} %param.30) | copy-start | bytes 772
  7.2 141.0 %all-gather.2.cloned.1.call-start = ((), (), s32[]{:S(2)}) async-start(), calls=%async_computation.2 | async-start | bytes 4718592 | tf_op jit(solution)/shard_map/all_gather | solution.py:174
  11.1 13.6 %copy-start.12 = (bf16[2,32,32]{2,1,0:T(8,128)(2,1)}, bf16[2,32,32]{2,1,0:T(8,128)(2,1)S(1)}, u32[]{:S(2)}) copy-start(bf16[2,32,32]{2,1,0:T(8,128)(2,1)S(1)} %convolution_convert_fusion) | copy-start | bytes 12292
  13.2 13.1 %copy-start.34 = (pred[2,32]{1,0:T(4,128)(4,1)}, pred[2,32]{1,0:T(4,128)(4,1)S(1)}, u32[]{:S(2)}) copy-start(pred[2,32]{1,0:T(4,128)(4,1)S(1)} %get-tuple-element.17) | copy-start | bytes 196
  13.2 13.0 %copy-start.31 = (s32[2,32]{1,0:T(2,128)}, s32[2,32]{1,0:T(2,128)S(1)}, u32[]{:S(2)}) copy-start(s32[2,32]{1,0:T(2,128)S(1)} %get-tuple-element.20) | copy-start | bytes 772
  13.9 10.8 %copy-start.19 = (pred[2]{0:T(512)(128)(4,1)}, pred[2]{0:T(512)(128)(4,1)S(1)}, u32[]{:S(2)}) copy-start(pred[2]{0:T(512)(128)(4,1)S(1)} %get-tuple-element.3) | copy-start | bytes 10
  13.9 7.1 %copy-start.27 = (s32[1024]{0:T(1024)}, s32[1024]{0:T(1024)S(1)}, u32[]{:S(2)}) copy-start(s32[1024]{0:T(1024)S(1)} %pad_clamp_fusion) | copy-start | bytes 12292
  15.7 8.4 %copy-start.11 = (bf16[4,4096]{1,0:T(4,128)(2,1)S(1)}, bf16[4,4096]{1,0:T(4,128)(2,1)}, u32[]{:S(2)}) copy-start(bf16[4,4096]{1,0:T(4,128)(2,1)} %param.28) | copy-start | bytes 98308
  17.4 7.6 %copy-start.4 = (bf16[2,3,4096]{2,0,1:T(2,128)(2,1)S(1)}, bf16[2,3,4096]{2,0,1:T(2,128)(2,1)}, u32[]{:S(2)}) copy-start(bf16[2,3,4096]{2,0,1:T(2,128)(2,1)} %param.26) | copy-start | bytes 147460
  20.7 2.4 %copy-start.17 = (pred[2,32,32]{2,1,0:T(8,128)(4,1)}, pred[2,32,32]{2,1,0:T(8,128)(4,1)S(1)}, u32[]{:S(2)}) copy-start(pred[2,32,32]{2,1,0:T(8,128)(4,1)S(1)} %copy.49) | copy-start | bytes 6148
  21.0 0.8 copy-start.9
  25.0 2.7 %copy-start.8 = (f32[2,32,1024]{2,1,0:T(8,128)S(1)}, f32[2,32,1024]{2,1,0:T(8,128)}, u32[]{:S(2)}) copy-start(f32[2,32,1024]{2,1,0:T(8,128)} %fusion.59) | copy-start | bytes 786436
  25.0 2.7 %copy-start.20 = (pred[2]{0:T(512)(128)(4,1)S(1)}, pred[2]{0:T(512)(128)(4,1)}, u32[]{:S(2)}) copy-start(pred[2]{0:T(512)(128)(4,1)} %copy-done.19) | copy-start | bytes 10
  25.0 2.7 %copy-start.32 = (f32[1,4,2,128]{3,1,2,0:T(4,128)S(1)}, f32[1,4,2,128]{3,1,2,0:T(4,128)}, u32[]{:S(2)}) copy-start(f32[1,4,2,128]{3,1,2,0:T(4,128)} %copy.73) | copy-start | bytes 12292
  25.0 2.7 %copy-start.33 = (f32[1,4,2,128]{3,1,2,0:T(4,128)S(1)}, f32[1,4,2,128]{3,1,2,0:T(4,128)}, u32[]{:S(2)}) copy-start(f32[1,4,2,128]{3,1,2,0:T(4,128)} %copy.74) | copy-start | bytes 12292
  32.3 14.7 %copy-start.13 = (bf16[2,32,32]{2,1,0:T(8,128)(2,1)S(1)}, bf16[2,32,32]{2,1,0:T(8,128)(2,1)}, u32[]{:S(2)}) copy-start(bf16[2,32,32]{2,1,0:T(8,128)(2,1)} %copy-done.12) | copy-start | bytes 12292
  32.3 14.7 %copy-start.16 = (f32[1,4096]{1,0:T(1,128)S(1)}, f32[1,4096]{1,0:T(1,128)}, u32[]{:S(2)}) copy-start(f32[1,4096]{1,0:T(1,128)} %get-tuple-element.9) | copy-start | bytes 49156
  32.3 14.7 %copy-start.21 = (pred[2]{0:T(512)(128)(4,1)S(1)}, pred[2]{0:T(512)(128)(4,1)}, u32[]{:S(2)}) copy-start(pred[2]{0:T(512)(128)(4,1)} %copy-done.19) | copy-start | bytes 10
  47.0 0.7 copy-start.15
  47.0 1.2 copy-start.3
  47.0 1.2 copy-start.24
  47.0 1.2 copy-start.25
  47.0 1.2 copy-start.30
  49.9 2.3 %copy-start.7 = (f32[2,32,32,2]{2,1,3,0:T(8,128)S(1)}, f32[2,32,32,2]{2,1,3,0:T(8,128)}, u32[]{:S(2)}) copy-start(f32[2,32,32,2]{2,1,3,0:T(8,128)} %copy.48) | copy-start | bytes 49156
  49.9 2.5 %copy-start.5 = (f32[2,32,64]{1,2,0:T(8,128)S(1)}, f32[2,32,64]{1,2,0:T(8,128)}, u32[]{:S(2)}) copy-start(f32[2,32,64]{1,2,0:T(8,128)} %copy.55) | copy-start | bytes 49156
  49.9 2.5 %copy-start.6 = (f32[2,32,64]{1,2,0:T(8,128)S(1)}, f32[2,32,64]{1,2,0:T(8,128)}, u32[]{:S(2)}) copy-start(f32[2,32,64]{1,2,0:T(8,128)} %copy.53) | copy-start | bytes 49156
  49.9 2.6 %copy-start.18 = (pred[2,32,32]{2,1,0:T(8,128)(4,1)S(1)}, pred[2,32,32]{2,1,0:T(8,128)(4,1)}, u32[]{:S(2)}) copy-start(pred[2,32,32]{2,1,0:T(8,128)(4,1)} %copy-done.17) | copy-start | bytes 6148
  49.9 2.6 %copy-start.37 = (f32[64]{0:T(128)S(1)}, f32[64]{0:T(128)}, u32[]{:S(2)}) copy-start(f32[64]{0:T(128)} %param.32) | copy-start | bytes 772
  52.1 1.6 copy-start.2
  61.2 2.1 %copy-start.22 = (pred[2]{0:T(512)(128)(4,1)S(1)}, pred[2]{0:T(512)(128)(4,1)}, u32[]{:S(2)}) copy-start(pred[2]{0:T(512)(128)(4,1)} %copy-done.19) | copy-start | bytes 10
  66.8 3.8 %copy-start.14 = (f32[4096]{0:T(1024)S(1)}, f32[4096]{0:T(1024)}, u32[]{:S(2)}) copy-start(f32[4096]{0:T(1024)} %convert_element_type.183) | copy-start | bytes 49156
  66.9 3.8 %copy-start.38 = (pred[2,32]{1,0:T(4,128)(4,1)S(1)}, pred[2,32]{1,0:T(4,128)(4,1)}, u32[]{:S(2)}) copy-start(pred[2,32]{1,0:T(4,128)(4,1)} %iota_compare_fusion.9) | copy-start | bytes 196
  72.0 100.0 %reduce-scatter.2.cloned.1.call-start = ((), (), s32[]{:S(2)}) async-start(), calls=%async_computation.3 | async-start | bytes 3145728 | tf_op jit(solution)/shard_map/reduce_scatter | solution.py:181
  172.0 5.6 %copy-start.10 = (f32[2,32,64]{2,1,0:T(8,128)S(1)}, f32[2,32,64]{2,1,0:T(8,128)}, u32[]{:S(2)}) copy-start(f32[2,32,64]{2,1,0:T(8,128)} %copy-done.9) | copy-start | bytes 49156
  172.0 5.6 %copy-start.35 = (pred[2,32,1]{1,0,2:T(4,128)(4,1)S(1)}, pred[2,32,1]{1,0,2:T(4,128)(4,1)}, u32[]{:S(2)}) copy-start(pred[2,32,1]{1,0,2:T(4,128)(4,1)} %get-tuple-element.22) | copy-start | bytes 196
  174.1 17.5 %all-to-all-start = ((bf16[8,2,16,1024]{3,2,1,0:T(8,128)(2,1)}), bf16[8,2,16,1024]{3,2,1,0:T(8,128)(2,1)S(1)}, u32[]{:S(2)}, u32[]{:S(2)}) async-start(bf16[8,2,16,1024]{3,2,1,0:T(8,128)(2,1)} %convert_element_type.185), calls=%async_computation.1 | async-start | bytes 1048576 | tf_op jit(solution)/shard_map/all_to_all | solution.py:184
  177.8 15.2 %copy-start.1 = (bf16[2,32,4096]{2,1,0:T(8,128)(2,1)S(1)}, bf16[2,32,4096]{2,1,0:T(8,128)(2,1)}, u32[]{:S(2)}) copy-start(bf16[2,32,4096]{2,1,0:T(8,128)(2,1)} %param.19) | copy-start | bytes 1572868
Sparse Core Ops, SparseCore 0:
  72.1 76.0 all-gather.1
  158.9 7.8 reduce-scatter.1
where the time goes:
time: 201 us; the launch traced here: 200 us
  waiting for transfers between devices  79.8 us (40%)
  matrix products  55 us (27%)
  local copies, waits for them, and re-layouts  26.6 us (13%)
  other arithmetic  19.9 us (10%)
  between operations  14.8 us (7%)
  starting transfers between devices  3.79 us (2%)
    all_gather x1, waiting for transfers between devices, local(): lax.all_gather(flat_rows, 'req', axis=0, tiled=True)  76 us
    dot_general x1, matrix products, tree_layer(): jnp.einsum('rngs,rgkps->rngkp', queries, state_grouped, precision=highest)  14.6 us
    dot_general x1, matrix products, tree_layer(): jnp.einsum('rjgkp,rjgs->rgkps', scaled, key_rows, precision=highest)  11.1 us
    dot_general x1, matrix products, local(): jnp.dot(lax.all_gather(flat_rows, 'req', axis=0, tiled=True), out_weight,...  10.5 us
    add x1, other arithmetic, tree_layer(): final_state = jnp.exp(last_level)[:, :, None, None] * cached_state + update  10.1 us
    dot_general x1, matrix products, tree_layer(): jnp.einsum('rnjh,rjhp->rnhp', weights, values, precision=highest)  4.98 us
    dot_general x6, matrix products, tree_conv(): jnp.einsum('rnj,rjc->rnc', shifts[lookback - 1], values, preferred_elemen...  4.39 us
    reshape x2, local copies, waits for them, and re-layouts, tree_layer(): values = conv_values.reshape(req_count, node_count, head_count, head_dim)  4.23 us
  transfers between devices with their start and end apart: 3, of which 2 were waited for; matrix products, arithmetic and copies ran while one was open for 12% of the time, Pallas kernels for 0%

commit v1 on v0

v1 whole, which is shorter than its diff:
```python
import functools

import jax
import jax.numpy as jnp
from jax import lax
from jax.experimental import pallas as pl
from jax.experimental.pallas import tpu as pltpu
from jax.sharding import PartitionSpec as P

f32 = jnp.float32
bf16 = jnp.bfloat16
highest = lax.Precision.HIGHEST
norm_epsilon = 1e-05
MESH = pl.DeviceIdType.MESH
NT = (((1,), (1,)), ((), ()))
TN = (((0,), (0,)), ((), ()))


def iota(shape, dim):
    return lax.broadcasted_iota(jnp.int32, shape, dim)


def dot(a, b):
    return jnp.dot(a, b, preferred_element_type=f32)


def silu(x):
    return x / (1.0 + jnp.exp(-x))


def spread(x, onehot, terms):
    total = None
    for _ in range(terms):
        part = x.astype(bf16)
        x = x - part.astype(f32)
        term = dot(part, onehot)
        total = term if total is None else total + term
    return total


def ssm_kernel(
    slot_s, size_s, parent_s,
    val_ref, gate_ref, kq_ref, step_ref, vcache_ref, kqcache_ref, vw_ref, kqw_ref,
    bias_ref, rate_ref, skip_ref, gain_ref, state_ref,
    hid_ref, unpack_ref, final_ref,
    shift_sc, anc_sc, depth_sc, last_sc, level_sc, size_sc, skip_sc, chan_sc, lane_sc,
):
    g = pl.program_id(0)
    r = pl.program_id(1)
    N = gate_ref.shape[1]
    H = skip_sc.shape[2]
    C = gate_ref.shape[2]
    PD = C // H
    half = N // 2
    slots = [lax.rem(slot_s[k], 2) for k in range(2)]

    @pl.when((g == 0) & (r == 0))
    def _():
        M = 2 * N
        rows, cols = iota((M, M), 0), iota((M, M), 1)
        par = jnp.full((M, M), -1, jnp.int32)
        for k in range(2):
            for n in range(1, N):
                par = jnp.where(rows == k * N + n, parent_s[k, n] + k * N, par)
        one = jnp.where(par == cols, 1.0, 0.0).astype(f32)
        eye = jnp.where(rows == cols, 1.0, 0.0).astype(f32)
        step_b = one.astype(bf16)
        second = dot(step_b, step_b)
        third = dot(second.astype(bf16), step_b)
        anc = eye + one
        power = second
        reach = 2
        while reach < N:
            anc = dot(anc.astype(bf16), (eye + power).astype(bf16))
            reach *= 2
            if reach < N:
                power = dot(power.astype(bf16), power.astype(bf16))
        for k in range(2):
            lo, hi = k * N, (k + 1) * N
            for i, mat in enumerate((one, second, third)):
                tile = jnp.where(
                    iota((M, N), 0) - iota((M, N), 1) == lo, 1.0, 0.0
                ).astype(bf16)
                shift_sc[k, i * N:(i + 1) * N, :] = dot(mat[lo:hi].astype(bf16), tile).astype(bf16)
        fold = jnp.where(lax.rem(iota((M, 4 * N), 0), N) == lax.rem(iota((M, 4 * N), 1), N), 1.0, 0.0)
        anc_sc[...] = dot(anc.astype(bf16), fold.astype(bf16))
        depth_sc[...] = jnp.broadcast_to(jnp.sum(anc, axis=1, keepdims=True) - 1.0, depth_sc.shape)
        row_h = iota((M, H), 0)
        pick = (row_h == size_s[0] - 1) | (row_h == N + size_s[1] - 1)
        last_sc[...] = lax.dot_general(
            anc.astype(bf16), jnp.where(pick, 1.0, 0.0).astype(bf16), TN, preferred_element_type=f32
        )
        x = jnp.concatenate([step_ref[slots[0]], step_ref[slots[1]]], axis=0).astype(f32) + bias_ref[...]
        step = jnp.maximum(x, 0.0) + jnp.log1p(jnp.exp(-jnp.abs(x)))
        rate = -jnp.exp(rate_ref[...])
        level = jnp.dot(anc, step * rate, precision=highest, preferred_element_type=f32)
        for k in range(2):
            level_sc[k] = level[:, k * H:(k + 1) * H]
            size_sc[k] = step[:, k * H:(k + 1) * H]
            skip_sc[k] = jnp.broadcast_to(skip_ref[:, k * H:(k + 1) * H], skip_sc.shape[1:])
        chan_sc[...] = jnp.where(iota((H, C), 1) // PD == iota((H, C), 0), 1.0, 0.0).astype(bf16)
        lane_sc[...] = jnp.where(iota((H, H * N), 1) // N == iota((H, H * N), 0), 1.0, 0.0).astype(bf16)
        u_row, u_col = iota((N, half), 0), iota((N, half), 1)
        req = u_row // half
        node = u_row - req * half
        over = jnp.maximum(size_s[0] - half, 0)
        place = node + jnp.where(req == 1, over, 0)
        live = node + half < jnp.where(req == 1, size_s[1], size_s[0])
        unpack_ref[...] = jnp.where((u_col == place) & live, 1.0, 0.0).astype(bf16)

    slot = lax.rem(slot_s[r], 2)
    own = pl.ds(pl.multiple_of(r * N, N), N)
    depth = depth_sc[own, 0:1]
    shifts = shift_sc[r]

    def conv(x, cache, w):
        w = w.astype(f32)
        cache = cache.astype(f32)
        back = dot(shifts, x)
        total = w[3:4] * x.astype(f32)
        for k in range(1, 4):
            total = total + w[3 - k:4 - k] * back[(k - 1) * N:k * N]
        c0, c1, c2 = cache[0:1], cache[1:2], cache[2:3]
        w0, w1, w2 = w[0:1], w[1:2], w[2:3]
        total = total + jnp.where(depth == 0.0, w2 * c2 + w1 * c1 + w0 * c0, 0.0)
        total = total + jnp.where(depth == 1.0, w1 * c2 + w0 * c1, 0.0)
        total = total + jnp.where(depth == 2.0, w0 * c2, 0.0)
        return silu(total)

    kq = conv(kq_ref[slot], kqcache_ref[r], kqw_ref[...])
    S = kq.shape[1] // 2
    key, query = kq[:, :S], kq[:, S:]
    key_b, query_b = key.astype(bf16), query.astype(bf16)
    level = level_sc[g, own, :]
    step = size_sc[g, own, :]
    m = size_s[r] - 1
    level_m = jnp.sum(jnp.where(iota((N, H), 0) == m, level, 0.0), axis=0, keepdims=True)
    last_decay = jnp.exp(jnp.where(last_sc[own, :] > 0.5, level_m - level, -1e30))
    decay_m = jnp.exp(level_m)
    stacked = jnp.concatenate([step, jnp.exp(level), last_decay, skip_sc[g]], axis=0)
    wide = spread(stacked, chan_sc[...], 2)
    level_x = spread(level, lane_sc[...], 3)
    diag = lax.rem(iota((N, H * N), 1), N) == iota((N, H * N), 0)
    level_row = jnp.sum(jnp.where(diag, level_x, 0.0), axis=0, keepdims=True)
    anc4 = anc_sc[own, :] > 0.5
    key4 = jnp.concatenate([key] * 4, axis=0)
    affinity4 = lax.dot_general(query, key4, NT, precision=highest, preferred_element_type=f32)
    block_mask = iota((4 * N, 4 * PD), 0) // N == iota((4 * N, 4 * PD), 1) // PD

    pieces = []
    for q in range(H // 4):
        cs = slice(q * 4 * PD, (q + 1) * 4 * PD)
        ls = slice(q * 4 * N, (q + 1) * 4 * N)
        values = conv(val_ref[slot, :, cs], vcache_ref[r, :, cs], vw_ref[:, cs])
        gap = level_x[:, ls] - level_row[:, ls]
        weights = affinity4 * jnp.exp(jnp.where(anc4, gap, -1e30))
        stepped = values * wide[0:N, cs]
        four = jnp.concatenate([stepped] * 4, axis=0)
        four = jnp.where(block_mask, four, 0.0).astype(bf16)
        inner = dot(weights.astype(bf16), four)
        state = state_ref[0, 4 * q:4 * q + 4].reshape(4 * PD, S)
        carried = lax.dot_general(query_b, state.astype(bf16), NT, preferred_element_type=f32)
        result = inner + carried * wide[N:2 * N, cs] + wide[3 * N:3 * N + 1, cs] * values
        pieces.append(result * silu(gate_ref[slot, :, cs].astype(f32)))
        scaled = (stepped * wide[2 * N:3 * N, cs]).astype(bf16)
        update = lax.dot_general(scaled, key_b, TN, preferred_element_type=f32)
        for k in range(4):
            h = 4 * q + k
            final_ref[0, h] = (
                jnp.broadcast_to(decay_m[:, h:h + 1], (PD, S)) * state_ref[0, h]
                + update[k * PD:(k + 1) * PD]
            )
    square = sum(jnp.sum(p * p, axis=1, keepdims=True) for p in pieces)
    inverse = lax.rsqrt(square / C + norm_epsilon)
    live = iota((N, 1), 0) < size_s[r]
    a_row, a_col = iota((half, half), 0), iota((half, half), 1)
    over = jnp.where(r == 1, jnp.maximum(size_s[0] - half, 0), 0)
    pack = jnp.where(a_row == a_col + over, 1.0, 0.0).astype(bf16)
    for q, piece in enumerate(pieces):
        cs = slice(q * 4 * PD, (q + 1) * 4 * PD)
        normed = piece * inverse * gain_ref[:, cs].astype(f32)
        hidden = jnp.where(live, normed, 0.0).astype(bf16)
        hid_ref[0, pl.ds(pl.multiple_of(r * half, half), half), cs] = hidden[:half]
        tail = dot(pack, hidden[half:])

        @pl.when(r == 0)
        def _():
            hid_ref[0, N:, cs] = tail.astype(bf16)

        @pl.when(r == 1)
        def _():
            hid_ref[0, N:, cs] = (hid_ref[0, N:, cs].astype(f32) + tail).astype(bf16)


def comm_kernel(
    R, packed, unpack, w_any, out,
    wbuf, gath, part, other, fin, back,
    w_sem, send_sem, recv_sem, ex_send, ex_recv, home_send, home_recv,
):
    gi, me, c = lax.axis_index("group"), lax.axis_index("req"), lax.axis_index("chan")
    A = R // 2
    a = me // 2
    b = me - 2 * a
    pair = 2 * a + 1 - b
    cols = wbuf.shape[1]
    rows = gath.shape[2]
    low = out.shape[1] * 2
    wcopy = pltpu.make_async_copy(w_any, wbuf, w_sem)
    wcopy.start()

    barrier = pltpu.get_barrier_semaphore()
    for k in range(1, R):
        pl.semaphore_signal(barrier, inc=1, device_id=(gi, lax.rem(me + k, R), c), device_id_type=MESH)
    pl.semaphore_signal(barrier, inc=1, device_id=(gi, me, 1 - c), device_id_type=MESH)
    pl.semaphore_wait(barrier, R)

    def push(src, way, slot, u, target):
        return pltpu.make_async_remote_copy(
            src_ref=src, dst_ref=gath.at[slot, u],
            send_sem=send_sem.at[way, slot, u], recv_sem=recv_sem.at[slot, u],
            device_id=(gi, target, c), device_id_type=MESH,
        )

    def arrived(slot, u):
        push(gath.at[slot, u], 0, slot, u, pair).wait_recv()

    def exchange(slot, lo, hi):
        return pltpu.make_async_remote_copy(
            src_ref=part.at[slot, lo:hi], dst_ref=other.at[slot, lo:hi],
            send_sem=ex_send.at[slot], recv_sem=ex_recv.at[slot],
            device_id=(gi, me, 1 - c), device_id_type=MESH,
        )

    def home(slot, place, target, lo, hi):
        return pltpu.make_async_remote_copy(
            src_ref=fin.at[slot, lo:hi], dst_ref=back.at[place, lo:hi],
            send_sem=home_send.at[slot], recv_sem=home_recv.at[place],
            device_id=(gi, target, c), device_id_type=MESH,
        )

    def by_core(fn):
        @pl.when(c == 0)
        def _():
            fn((0, low), (low, rows))

        @pl.when(c == 1)
        def _():
            fn((low, rows), (0, low))

    depth = gath.shape[3]

    def multiply(slot, first, second):
        @pl.loop(0, cols // 256)
        def _(t):
            at = pl.ds(pl.multiple_of(t * 256, 256), 256)
            part[slot, :, at] = dot(first[...], wbuf[:depth, at]) + dot(second[...], wbuf[depth:, at])
        by_core(lambda mine, theirs: exchange(slot, *theirs).start())

    def finish(slot):
        def fn(mine, theirs):
            exchange(slot, *mine).wait_recv()
            at = slice(*mine)
            fin[slot, at] = (part[slot, at] + other[slot, at]).astype(bf16)
            home(slot, me, slot, *mine).start()
        by_core(fn)

    for u in range(2):
        @pl.when(a < A - 1)
        def _():
            push(packed.at[u], 0, me, u, me + 2).start()

        @pl.when(a > 0)
        def _():
            push(packed.at[u], 1, me, u, me - 2).start()
        push(packed.at[u], 2, me, u, pair).start()

    wcopy.wait()
    multiply(me, packed.at[0], packed.at[1])

    def finish_own(mine, theirs):
        exchange(me, *mine).wait_recv()
        at = slice(*mine)
        back[me, at] = (part[me, at] + other[me, at]).astype(bf16)
    by_core(finish_own)

    def step(t, carry):
        left, right = a - t, a + t
        pleft, pright = a - t + 1, a + t - 1
        for u in range(2):
            @pl.when(left >= 0)
            def _():
                s = 2 * left + b
                arrived(s, u)

                @pl.when(a < A - 1)
                def _():
                    push(gath.at[s, u], 0, s, u, me + 2).start()
                push(gath.at[s, u], 2, s, u, pair).start()

            @pl.when(right < A)
            def _():
                s = 2 * right + b
                arrived(s, u)

                @pl.when(a > 0)
                def _():
                    push(gath.at[s, u], 1, s, u, me - 2).start()
                push(gath.at[s, u], 2, s, u, pair).start()
        work = (
            (left >= 0, 2 * left + b, False),
            (right < A, 2 * right + b, False),
            (pleft >= 0, 2 * pleft + 1 - b, True),
            ((pright < A) & (t > 1), 2 * pright + 1 - b, True),
        )
        for valid, s, wait in work:
            @pl.when(valid)
            def _():
                if wait:
                    arrived(s, 0)
                    arrived(s, 1)
                multiply(s, gath.at[s, 0], gath.at[s, 1])
        for valid, s, wait in work:
            @pl.when(valid)
            def _():
                finish(s)
        return carry

    lax.fori_loop(1, A + 1, step, 0)

    def place(s, carry):
        at = pl.ds(pl.multiple_of(s * cols, cols), cols)

        def wait(mine, theirs):
            @pl.when(s != me)
            def _():
                home(s, s, s, *mine).wait_recv()
        by_core(wait)

        @pl.when(c == 0)
        def _():
            out[0, :, at] = back[s, :low // 2]
            out[1, :, at] = back[s, low // 2:low]

        @pl.when(c == 1)
        def _():
            both = dot(unpack[...], back[s, low:]).astype(bf16)
            out[0, :, at] = both[:low // 2]
            out[1, :, at] = both[low // 2:]
        return carry

    lax.fori_loop(0, R, place, 0)

    def drain(s, carry):
        sa = s // 2
        mine_col = s - 2 * sa == b

        def fn(mine, theirs):
            exchange(s, *theirs).wait_send()

            @pl.when(s != me)
            def _():
                home(s, me, s, *mine).wait_send()
        by_core(fn)
        for u in range(2):
            @pl.when(mine_col & (sa <= a) & (a < A - 1))
            def _():
                push(packed.at[u], 0, s, u, me + 2).wait_send()

            @pl.when(mine_col & (sa >= a) & (a > 0))
            def _():
                push(packed.at[u], 1, s, u, me - 2).wait_send()

            @pl.when(mine_col)
            def _():
                push(packed.at[u], 2, s, u, pair).wait_send()
        return carry

    lax.fori_loop(0, R, drain, 0)


def local(
    value_stream, gate_stream, key_query_stream, step_stream, parents, tree_sizes, slot_index,
    value_cache, key_query_cache, value_conv, key_query_conv, step_bias, log_rate, skip_gain,
    norm_gain, cached_state, out_weight,
):
    Q, N, C = value_stream.shape
    G = key_query_stream.shape[2]
    heads, PD, S = cached_state.shape[1:]
    H = heads // G
    CG = C // G
    R = lax.axis_size("req")
    packed_rows = N + N // 2
    kq = key_query_stream.reshape(Q, N, -1)
    kq_cache = key_query_cache.reshape(Q, 3, -1)
    kq_conv = key_query_conv.reshape(key_query_conv.shape[0], -1)
    smem = pl.BlockSpec(memory_space=pltpu.SMEM)
    whole = lambda x: pl.BlockSpec(x.shape, lambda g, r: (0,) * x.ndim)
    by_group = lambda x, n: pl.BlockSpec(x.shape[:-1] + (n,), lambda g, r: (0,) * (x.ndim - 1) + (g,))
    bias, rate, skip = (x.reshape(1, -1) for x in (step_bias, log_rate, skip_gain))
    gain = norm_gain.reshape(1, -1)
    state_spec = pl.BlockSpec((1, H, PD, S), lambda g, r: (r, g, 0, 0))
    packed, unpack, final_state = pl.pallas_call(
        ssm_kernel,
        grid=(G, Q),
        out_shape=(
            jax.ShapeDtypeStruct((G, packed_rows, CG), bf16),
            jax.ShapeDtypeStruct((N, N // 2), bf16),
            jax.ShapeDtypeStruct(cached_state.shape, f32),
        ),
        in_specs=[
            smem, smem, smem,
            by_group(value_stream, CG), by_group(gate_stream, CG), by_group(kq, 2 * S), whole(step_stream),
            by_group(value_cache, CG), by_group(kq_cache, 2 * S), by_group(value_conv, CG),
            by_group(kq_conv, 2 * S), whole(bias), whole(rate), whole(skip), by_group(gain, CG), state_spec,
        ],
        out_specs=(
            pl.BlockSpec((1, packed_rows, CG), lambda g, r: (g, 0, 0)),
            pl.BlockSpec((N, N // 2), lambda g, r: (0, 0)),
            state_spec,
        ),
        scratch_shapes=[
            pltpu.VMEM((2, 3 * N, N), bf16),
            pltpu.VMEM((2 * N, 4 * N), f32),
            pltpu.VMEM((2 * N, 128), f32),
            pltpu.VMEM((2 * N, H), f32),
            pltpu.VMEM((2, 2 * N, H), f32),
            pltpu.VMEM((2, 2 * N, H), f32),
            pltpu.VMEM((2, 8, H), f32),
            pltpu.VMEM((H, CG), bf16),
            pltpu.VMEM((H, H * N), bf16),
        ],
        compiler_params=pltpu.CompilerParams(vmem_limit_bytes=40 * 2**20),
        name="ssm",
    )(
        slot_index, tree_sizes, parents, value_stream, gate_stream, kq, step_stream, value_cache,
        kq_cache, value_conv, kq_conv, bias, rate, skip, gain, cached_state,
    )
    cols = out_weight.shape[1]
    vmem = pl.BlockSpec(memory_space=pltpu.VMEM)
    dma = pltpu.SemaphoreType.DMA
    out = pl.pallas_call(
        functools.partial(comm_kernel, R),
        out_shape=jax.ShapeDtypeStruct((Q, N // 2, R * cols), bf16),
        in_specs=[vmem, vmem, pl.BlockSpec(memory_space=pl.ANY)],
        out_specs=vmem,
        scratch_shapes=[
            pltpu.VMEM(out_weight.shape, bf16),
            pltpu.VMEM((R, G, packed_rows, CG), bf16),
            pltpu.VMEM((R, packed_rows, cols), f32),
            pltpu.VMEM((R, packed_rows, cols), f32),
            pltpu.VMEM((R, packed_rows, cols), bf16),
            pltpu.VMEM((R, packed_rows, cols), bf16),
            dma, dma((3, R, G)), dma((R, G)), dma((R,)), dma((R,)), dma((R,)), dma((R,)),
        ],
        compiler_params=pltpu.CompilerParams(
            collective_id=0, has_side_effects=True, vmem_limit_bytes=40 * 2**20
        ),
        name="project",
    )(packed, unpack, out_weight)
    return (out, final_state)


def solution(mesh):
    return jax.shard_map(
        local,
        mesh=mesh,
        in_specs=(
            P(("group", "req"), None, "chan"),
            P(("group", "req"), None, "chan"),
            P(("group", "req"), None, "chan", None),
            P(("group", "req"), None, "chan"),
            P(("group", "req"), None),
            P(("group", "req")),
            P(("group", "req")),
            P(("group", "req"), None, "chan"),
            P(("group", "req"), None, "chan", None),
            P(None, "chan"),
            P(None, "chan", None),
            P("chan"),
            P("chan"),
            P("chan"),
            P("chan"),
            P(("group", "req"), "chan", None, None),
            P("chan", "req"),
        ),
        out_specs=(P(("group", "req"), "chan", None), P(("group", "req"), "chan", None, None)),
        check_vma=False,
    )
```

time: 201 us -> 85.2 us (0.42)
  waiting for transfers between devices: 79.8 us -> 0 us
  Pallas kernels: 0 us -> 68.2 us
  matrix products: 55 us -> 0 us
  other arithmetic: 19.9 us -> 0 us
  between operations: 14.8 us -> 0.67 us
  local copies, waits for them, and re-layouts: 26.6 us -> 15.6 us
  starting transfers between devices: 3.79 us -> 0 us
    all_gather x1 -> x0, waiting for transfers between devices: 76 us -> none  [local(): lax.all_gather(flat_rows, 'req', axis=0, tiled=True)]
    pallas_call x0 -> x2, Pallas kernels: none -> 68.2 us  [the longest x1 52.6 us: local(): pl.pallas_call(functools.partial(comm_kernel, R), out_shape=jax.ShapeDtyp...]
    dot_general x29 -> x0, matrix products: 55 us -> none  [the longest x1 14.6 us: tree_layer(): jnp.einsum('rngs,rgkps->rngkp', queries, state_grouped, precision=highest)]
    add x2 -> x0, other arithmetic: 10.1 us -> none  [the longest x1 10.1 us: tree_layer(): final_state = jnp.exp(last_level)[:, :, None, None] * cached_state + update]
    unnamed x84 -> x27, local copies, waits for them, and re-layouts: 3.11 us -> 13.2 us
    mul x4 -> x0, local copies, waits for them, and re-layouts: 5.63 us -> none  [the longest x2 3.43 us: tree_layer(): blocks * inverse_rms]
    gather x5 -> x0, local copies, waits for them, and re-layouts: 4.79 us -> none  [the longest x2 1.79 us: local(): jnp.take(key_query_stream, slot_order, axis=0)]
    convert_element_type x6 -> x0, other arithmetic: 4.65 us -> none  [the longest x1 2.11 us: local(): shares = lax.psum_scatter(split_terms, 'chan', scatter_dimension=scatter_...]
  transfers between devices with their start and end apart: 3 -> 0, of which waited for: 2 -> 0; matrix products, arithmetic and copies ran while one was open for 12% -> 0% of each run, Pallas kernels for 0% -> 0%
where the time goes in v1:
time: 85.2 us; the launch traced here: 84.5 us
  Pallas kernels  68.2 us (80%)
  local copies, waits for them, and re-layouts  15.6 us (18%)
    pallas_call x1, Pallas kernels, local(): pl.pallas_call(functools.partial(comm_kernel, R), out_shape=jax.ShapeDtyp...  52.6 us
    pallas_call x1, Pallas kernels, local(): pl.pallas_call(ssm_kernel, grid=(G, Q), out_shape=(jax.ShapeDtypeStruct((...  15.5 us
    unnamed x27, local copies, waits for them, and re-layouts  13.2 us

profile of v1, /device:TPU:0, one launch (start us, length us, event | category | flops | bytes accessed | tf_op | source)
XLA Modules:
  0.0 84.5 jit_solution(17981750949701331876)
XLA Ops:
  0.6 0.7 copy.24
  1.3 0.7 reshape.32.kqcache_ref
  2.1 0.7 reshape.31.gain_ref
  2.8 0.8 %copy.21.vcache_ref = bf16[2,3,4096]{2,1,0:T(4,128)(2,1)S(1)} copy(bf16[2,3,4096]{2,0,1:T(2,128)(2,1)} %param.24) | data formatting | bytes 98304 | tf_op args[7]
  3.6 1.0 %reshape.25.kq_ref = bf16[2,32,1024]{2,1,0:T(8,128)(2,1)S(1)} reshape(bf16[2,32,2,512]{3,2,1,0:T(2,128)(2,1)} %param.19) | data formatting | bytes 262144 | tf_op jit(solution)/shard_map/reshape | solution.py:393
  4.6 0.0 copy-start
  4.6 3.4 %copy-done = f32[2,64,64,256]{3,2,1,0:T(8,128)S(1)} copy-done((f32[2,64,64,256]{3,2,1,0:T(8,128)S(1)}, f32[2,64,64,256]{3,2,1,0:T(8,128)}, u32[]{:S(2)}) %copy-start) | copy-done | bytes 8388632
  8.0 0.0 copy-start.2
  8.0 1.0 %copy-done.2 = bf16[2,32,4096]{2,1,0:T(8,128)(2,1)S(1)} copy-done((bf16[2,32,4096]{2,1,0:T(8,128)(2,1)S(1)}, bf16[2,32,4096]{2,1,0:T(8,128)(2,1)}, u32[]{:S(2)}) %copy-start.2) | copy-done | bytes 524312
  9.0 0.0 copy-start.3
  9.0 1.0 %copy-done.3 = bf16[2,32,4096]{2,1,0:T(8,128)(2,1)S(1)} copy-done((bf16[2,32,4096]{2,1,0:T(8,128)(2,1)S(1)}, bf16[2,32,4096]{2,1,0:T(8,128)(2,1)}, u32[]{:S(2)}) %copy-start.3) | copy-done | bytes 524312
  10.1 0.0 copy-start.4
  10.1 0.8 copy-done.4
  10.8 0.0 copy-start.5
  10.8 0.7 copy-done.5
  11.5 0.0 copy-start.6
  11.5 0.7 copy-done.6
  12.2 0.0 copy-start.7
  12.2 0.7 copy-done.7
  12.9 0.0 copy-start.8
  12.9 0.7 copy-done.8
  13.5 0.0 copy-start.9
  13.5 0.7 copy-done.9
  14.2 0.0 copy-start.10
  14.2 0.7 copy-done.10
  14.8 0.0 copy-start.11
  14.8 0.7 copy-done.11
  15.5 0.0 copy-start.1
  15.5 15.5 %ssm.1 = (bf16[2,48,2048]{2,1,0:T(8,128)(2,1)S(1)}, bf16[32,16]{1,0:T(8,128)(2,1)S(1)}, f32[2,64,64,256]{3,2,1,0:T(8,128)}) custom-call(s32[2]{0:T(128)S(1)} %copy-done.7, s32[2]{0:T(128)S(1)} %copy-done.8, s32[2,32]{1,0:T(2,128)S(1)} %copy-done.6, bf16[2,32,4096]{2,1,0:T(8,128)(2,1)S(1)} %copy-done.2, bf16[2,32,4096]{2,1,0:T(8,128)(2,1)S(1)} %copy-done.3, ...), custom_call_target="tpu_custom_call" | custom-call | tf_op jit(solution)/shard_map/ssm/pallas_call | solution.py:402
  31.0 0.0 copy-done.1
  31.1 52.6 %project.1 = bf16[2,16,8192]{2,1,0:T(8,128)(2,1)S(1)} custom-call(bf16[2,48,2048]{2,1,0:T(8,128)(2,1)S(1)} %get-tuple-element.5.packed, bf16[32,16]{1,0:T(8,128)(2,1)S(1)} %get-tuple-element.6.unpack, bf16[4096,1024]{1,0:T(8,128)(2,1)S(1)} %copy-done.1), custom_call_target="tpu_custom_call" | custom-call | tf_op jit(solution)/shard_map/project/pallas_call | solution.py:441
  83.7 0.8 copy.26
Async XLA Ops:
  4.6 3.4 %copy-start = (f32[2,64,64,256]{3,2,1,0:T(8,128)S(1)}, f32[2,64,64,256]{3,2,1,0:T(8,128)}, u32[]{:S(2)}) copy-start(f32[2,64,64,256]{3,2,1,0:T(8,128)} %state_ref.1) | copy-start | bytes 25165828
  8.0 1.0 %copy-start.2 = (bf16[2,32,4096]{2,1,0:T(8,128)(2,1)S(1)}, bf16[2,32,4096]{2,1,0:T(8,128)(2,1)}, u32[]{:S(2)}) copy-start(bf16[2,32,4096]{2,1,0:T(8,128)(2,1)} %val_ref.1) | copy-start | bytes 1572868
  9.0 1.0 %copy-start.3 = (bf16[2,32,4096]{2,1,0:T(8,128)(2,1)S(1)}, bf16[2,32,4096]{2,1,0:T(8,128)(2,1)}, u32[]{:S(2)}) copy-start(bf16[2,32,4096]{2,1,0:T(8,128)(2,1)} %gate_ref.1) | copy-start | bytes 1572868
  10.1 0.8 copy-start.4
  10.8 0.7 copy-start.5
  11.5 0.7 copy-start.6
  12.2 0.7 copy-start.7
  12.9 0.7 copy-start.8
  13.5 0.7 copy-start.9
  14.2 0.7 copy-start.10
  14.8 0.7 copy-start.11
  15.5 15.6 %copy-start.1 = (bf16[4096,1024]{1,0:T(8,128)(2,1)S(1)}, bf16[4096,1024]{1,0:T(8,128)(2,1)}, u32[]{:S(2)}) copy-start(bf16[4096,1024]{1,0:T(8,128)(2,1)} %w_any.1) | copy-start | bytes 25165828

commit v2 on v1

--- a/solution.py
+++ b/solution.py
@@ -114,20 +114,27 @@
     shifts = shift_sc[r]
 
     def conv(x, cache, w):
-        w = w.astype(f32)
-        cache = cache.astype(f32)
         back = dot(shifts, x)
-        total = w[3:4] * x.astype(f32)
+        c0, c1, c2 = cache
+        w0, w1, w2, w3 = w
+        total = w3 * x.astype(f32)
         for k in range(1, 4):
-            total = total + w[3 - k:4 - k] * back[(k - 1) * N:k * N]
-        c0, c1, c2 = cache[0:1], cache[1:2], cache[2:3]
-        w0, w1, w2 = w[0:1], w[1:2], w[2:3]
+            total = total + w[3 - k] * back[(k - 1) * N:k * N]
         total = total + jnp.where(depth == 0.0, w2 * c2 + w1 * c1 + w0 * c0, 0.0)
         total = total + jnp.where(depth == 1.0, w1 * c2 + w0 * c1, 0.0)
         total = total + jnp.where(depth == 2.0, w0 * c2, 0.0)
         return silu(total)
 
-    kq = conv(kq_ref[slot], kqcache_ref[r], kqw_ref[...])
+    def row_of(pair, index):
+        pair = pair.astype(f32)
+        return jnp.where(index == 0, pair[0:1], pair[1:2])
+
+    kq_rows = jnp.where(g == 0, kq_ref[slot, :, 0, :].astype(f32), kq_ref[slot, :, 1, :].astype(f32))
+    kq = conv(
+        kq_rows.astype(bf16),
+        [row_of(kqcache_ref[r, k], g) for k in range(3)],
+        [row_of(kqw_ref[k], g) for k in range(4)],
+    )
     S = kq.shape[1] // 2
     key, query = kq[:, :S], kq[:, S:]
     key_b, query_b = key.astype(bf16), query.astype(bf16)
@@ -151,7 +158,12 @@
     for q in range(H // 4):
         cs = slice(q * 4 * PD, (q + 1) * 4 * PD)
         ls = slice(q * 4 * N, (q + 1) * 4 * N)
-        values = conv(val_ref[slot, :, cs], vcache_ref[r, :, cs], vw_ref[:, cs])
+        taps = vw_ref[:, cs].astype(f32)
+        values = conv(
+            val_ref[slot, :, cs],
+            [row_of(vcache_ref[k, :, cs], r) for k in range(3)],
+            [taps[k:k + 1] for k in range(4)],
+        )
         gap = level_x[:, ls] - level_row[:, ls]
         weights = affinity4 * jnp.exp(jnp.where(anc4, gap, -1e30))
         stepped = values * wide[0:N, cs]
@@ -178,7 +190,7 @@
     pack = jnp.where(a_row == a_col + over, 1.0, 0.0).astype(bf16)
     for q, piece in enumerate(pieces):
         cs = slice(q * 4 * PD, (q + 1) * 4 * PD)
-        normed = piece * inverse * gain_ref[:, cs].astype(f32)
+        normed = piece * inverse * gain_ref[cs].astype(f32).reshape(1, -1)
         hidden = jnp.where(live, normed, 0.0).astype(bf16)
         hid_ref[0, pl.ds(pl.multiple_of(r * half, half), half), cs] = hidden[:half]
         tail = dot(pack, hidden[half:])
@@ -295,7 +307,10 @@
                 @pl.when(a < A - 1)
                 def _():
                     push(gath.at[s, u], 0, s, u, me + 2).start()
-                push(gath.at[s, u], 2, s, u, pair).start()
+
+                @pl.when((left > 0) | (u == 0))
+                def _():
+                    push(gath.at[s, u], 2, s, u, pair).start()
 
             @pl.when(right < A)
             def _():
@@ -305,21 +320,49 @@
                 @pl.when(a > 0)
                 def _():
                     push(gath.at[s, u], 1, s, u, me - 2).start()
-                push(gath.at[s, u], 2, s, u, pair).start()
+
+                @pl.when((right < A - 1) | (u == 0))
+                def _():
+                    push(gath.at[s, u], 2, s, u, pair).start()
+
+        @pl.when(left == -1)
+        def _():
+            s = 1 - b
+            arrived(s, 1)
+
+            @pl.when(a < A - 1)
+            def _():
+                push(gath.at[s, 1], 0, s, 1, me + 2).start()
+
+        @pl.when(right == A)
+        def _():
+            s = 2 * (A - 1) + 1 - b
+            arrived(s, 1)
+
+            @pl.when(a > 0)
+            def _():
+                push(gath.at[s, 1], 1, s, 1, me - 2).start()
         work = (
-            (left >= 0, 2 * left + b, False),
-            (right < A, 2 * right + b, False),
-            (pleft >= 0, 2 * pleft + 1 - b, True),
-            ((pright < A) & (t > 1), 2 * pright + 1 - b, True),
+            (left >= 0, left, b, False),
+            (right < A, right, b, False),
+            (pleft >= 0, pleft, 1 - b, True),
+            ((pright < A) & (t > 1), pright, 1 - b, True),
         )
-        for valid, s, wait in work:
+        for valid, place, column, wait in work:
+            s = 2 * place + column
+
             @pl.when(valid)
             def _():
                 if wait:
                     arrived(s, 0)
-                    arrived(s, 1)
+
+                    @pl.when((place > 0) & (place < A - 1))
+                    def _():
+                        arrived(s, 1)
                 multiply(s, gath.at[s, 0], gath.at[s, 1])
-        for valid, s, wait in work:
+        for valid, place, column, wait in work:
+            s = 2 * place + column
+
             @pl.when(valid)
             def _():
                 finish(s)
@@ -370,9 +413,19 @@
             def _():
                 push(packed.at[u], 1, s, u, me - 2).wait_send()
 
-            @pl.when(mine_col)
+            direct = (sa == a) | (u == 0) | ((sa > 0) & (sa < A - 1))
+
+            @pl.when(mine_col & direct)
             def _():
                 push(packed.at[u], 2, s, u, pair).wait_send()
+
+        @pl.when((s == 1 - b) & (a < A - 1))
+        def _():
+            push(packed.at[1], 0, s, 1, me + 2).wait_send()
+
+        @pl.when((s == 2 * (A - 1) + 1 - b) & (a > 0))
+        def _():
+            push(packed.at[1], 1, s, 1, me - 2).wait_send()
         return carry
 
     lax.fori_loop(0, R, drain, 0)
@@ -390,14 +443,11 @@
     CG = C // G
     R = lax.axis_size("req")
     packed_rows = N + N // 2
-    kq = key_query_stream.reshape(Q, N, -1)
-    kq_cache = key_query_cache.reshape(Q, 3, -1)
-    kq_conv = key_query_conv.reshape(key_query_conv.shape[0], -1)
+    caches = value_cache.transpose(1, 0, 2)
     smem = pl.BlockSpec(memory_space=pltpu.SMEM)
     whole = lambda x: pl.BlockSpec(x.shape, lambda g, r: (0,) * x.ndim)
     by_group = lambda x, n: pl.BlockSpec(x.shape[:-1] + (n,), lambda g, r: (0,) * (x.ndim - 1) + (g,))
     bias, rate, skip = (x.reshape(1, -1) for x in (step_bias, log_rate, skip_gain))
-    gain = norm_gain.reshape(1, -1)
     state_spec = pl.BlockSpec((1, H, PD, S), lambda g, r: (r, g, 0, 0))
     packed, unpack, final_state = pl.pallas_call(
         ssm_kernel,
@@ -409,9 +459,9 @@
         ),
         in_specs=[
             smem, smem, smem,
-            by_group(value_stream, CG), by_group(gate_stream, CG), by_group(kq, 2 * S), whole(step_stream),
-            by_group(value_cache, CG), by_group(kq_cache, 2 * S), by_group(value_conv, CG),
-            by_group(kq_conv, 2 * S), whole(bias), whole(rate), whole(skip), by_group(gain, CG), state_spec,
+            by_group(value_stream, CG), by_group(gate_stream, CG), whole(key_query_stream), whole(step_stream),
+            by_group(caches, CG), whole(key_query_cache), by_group(value_conv, CG),
+            whole(key_query_conv), whole(bias), whole(rate), whole(skip), pl.BlockSpec((CG,), lambda g, r: (g,)), state_spec,
         ],
         out_specs=(
             pl.BlockSpec((1, packed_rows, CG), lambda g, r: (g, 0, 0)),
@@ -429,11 +479,11 @@
             pltpu.VMEM((H, CG), bf16),
             pltpu.VMEM((H, H * N), bf16),
         ],
-        compiler_params=pltpu.CompilerParams(vmem_limit_bytes=40 * 2**20),
+        compiler_params=pltpu.CompilerParams(vmem_limit_bytes=60 * 2**20),
         name="ssm",
     )(
-        slot_index, tree_sizes, parents, value_stream, gate_stream, kq, step_stream, value_cache,
-        kq_cache, value_conv, kq_conv, bias, rate, skip, gain, cached_state,
+        slot_index, tree_sizes, parents, value_stream, gate_stream, key_query_stream, step_stream, caches,
+        key_query_cache, value_conv, key_query_conv, bias, rate, skip, norm_gain, cached_state,
     )
     cols = out_weight.shape[1]
     vmem = pl.BlockSpec(memory_space=pltpu.VMEM)
@@ -453,7 +503,7 @@
             dma, dma((3, R, G)), dma((R, G)), dma((R,)), dma((R,)), dma((R,)), dma((R,)),
         ],
         compiler_params=pltpu.CompilerParams(
-            collective_id=0, has_side_effects=True, vmem_limit_bytes=40 * 2**20
+            collective_id=0, has_side_effects=True, vmem_limit_bytes=60 * 2**20
         ),
         name="project",
     )(packed, unpack, out_weight)

time: 85.2 us -> 73.2 us (0.86)
  local copies, waits for them, and re-layouts: 15.6 us -> 1.87 us
  Pallas kernels: 68.2 us -> 70.5 us
    unnamed x27 -> x1, local copies, waits for them, and re-layouts: 13.2 us -> 1.87 us
    reshape x3 -> x0, local copies, waits for them, and re-layouts: 2.41 us -> none  [the longest x1 0.98 us: local(): kq = key_query_stream.reshape(Q, N, -1)]
    pallas_call x1, Pallas kernels: 15.5 us -> 17.2 us  [local(): pl.pallas_call(ssm_kernel, grid=(G, Q), out_shape=(jax.ShapeDtypeStruct((...]
where the time goes in v2:
time: 73.2 us; the launch traced here: 73 us
  Pallas kernels  70.5 us (96%)
  local copies, waits for them, and re-layouts  1.87 us (3%)
    pallas_call x1, Pallas kernels, local(): pl.pallas_call(functools.partial(comm_kernel, R), out_shape=jax.ShapeDtyp...  53.3 us
    pallas_call x1, Pallas kernels, local(): pl.pallas_call(ssm_kernel, grid=(G, Q), out_shape=(jax.ShapeDtypeStruct((...  17.2 us
    unnamed x1, local copies, waits for them, and re-layouts  1.87 us

profile of v2, /device:TPU:0, one launch (start us, length us, event | category | flops | bytes accessed | tf_op | source)
XLA Modules:
  0.0 73.0 jit_solution(12262349552248193531)
XLA Ops:
  0.6 17.2 %ssm.1 = (bf16[2,48,2048]{2,1,0:T(8,128)(2,1)}, bf16[32,16]{1,0:T(8,128)(2,1)}, f32[2,64,64,256]{3,2,1,0:T(8,128)}) custom-call(s32[2]{0:T(128)} %slot_s.1, s32[2]{0:T(128)} %size_s.1, s32[2,32]{1,0:T(2,128)} %parent_s.1, bf16[2,32,4096]{2,1,0:T(8,128)(2,1)} %val_ref.1, bf16[2,32,4096]{2,1,0:T(8,128)(2,1)} %gate_ref.1, bf16[2,32,2,512]{3,2,1,0:T(2,128)(2,1)} %kq_ref.1, ...), custom_call_target="tpu_custom_call" | custom-call | tf_op jit(solution)/shard_map/ssm/pallas_call | solution.py:452
  17.8 53.3 %project.1 = bf16[2,16,8192]{2,1,0:T(8,128)(2,1)} custom-call(bf16[2,48,2048]{2,1,0:T(8,128)(2,1)} %get-tuple-element.5.packed, bf16[32,16]{1,0:T(8,128)(2,1)} %get-tuple-element.6.unpack, bf16[4096,1024]{1,0:T(8,128)(2,1)} %w_any.1), custom_call_target="tpu_custom_call" | custom-call | tf_op jit(solution)/shard_map/project/pallas_call | solution.py:491
  71.1 1.9 %copy.20 = bf16[2,16,8192]{2,1,0:T(8,128)(2,1)} copy(bf16[2,16,8192]{2,1,0:T(8,128)(2,1)} %project.1) | data formatting | bytes 1048576

commit v3 on v2

--- a/solution.py
+++ b/solution.py
@@ -46,15 +46,14 @@
     shift_sc, anc_sc, depth_sc, last_sc, level_sc, size_sc, skip_sc, chan_sc, lane_sc,
 ):
     g = pl.program_id(0)
-    r = pl.program_id(1)
     N = gate_ref.shape[1]
     H = skip_sc.shape[2]
     C = gate_ref.shape[2]
     PD = C // H
     half = N // 2
-    slots = [lax.rem(slot_s[k], 2) for k in range(2)]
-
-    @pl.when((g == 0) & (r == 0))
+    slots = [lax.rem(slot_s[k], gate_ref.shape[0]) for k in range(2)]
+
+    @pl.when(g == 0)
     def _():
         M = 2 * N
         rows, cols = iota((M, M), 0), iota((M, M), 1)
@@ -108,12 +107,11 @@
         live = node + half < jnp.where(req == 1, size_s[1], size_s[0])
         unpack_ref[...] = jnp.where((u_col == place) & live, 1.0, 0.0).astype(bf16)
 
-    slot = lax.rem(slot_s[r], 2)
-    own = pl.ds(pl.multiple_of(r * N, N), N)
-    depth = depth_sc[own, 0:1]
-    shifts = shift_sc[r]
-
-    def conv(x, cache, w):
+    def row_of(pair, index):
+        pair = pair.astype(f32)
+        return jnp.where(index == 0, pair[0:1], pair[1:2])
+
+    def conv(x, cache, w, shifts, depth):
         back = dot(shifts, x)
         c0, c1, c2 = cache
         w0, w1, w2, w3 = w
@@ -125,83 +123,95 @@
         total = total + jnp.where(depth == 2.0, w0 * c2, 0.0)
         return silu(total)
 
-    def row_of(pair, index):
-        pair = pair.astype(f32)
-        return jnp.where(index == 0, pair[0:1], pair[1:2])
-
-    kq_rows = jnp.where(g == 0, kq_ref[slot, :, 0, :].astype(f32), kq_ref[slot, :, 1, :].astype(f32))
-    kq = conv(
-        kq_rows.astype(bf16),
-        [row_of(kqcache_ref[r, k], g) for k in range(3)],
-        [row_of(kqw_ref[k], g) for k in range(4)],
-    )
-    S = kq.shape[1] // 2
-    key, query = kq[:, :S], kq[:, S:]
-    key_b, query_b = key.astype(bf16), query.astype(bf16)
-    level = level_sc[g, own, :]
-    step = size_sc[g, own, :]
-    m = size_s[r] - 1
-    level_m = jnp.sum(jnp.where(iota((N, H), 0) == m, level, 0.0), axis=0, keepdims=True)
-    last_decay = jnp.exp(jnp.where(last_sc[own, :] > 0.5, level_m - level, -1e30))
-    decay_m = jnp.exp(level_m)
-    stacked = jnp.concatenate([step, jnp.exp(level), last_decay, skip_sc[g]], axis=0)
-    wide = spread(stacked, chan_sc[...], 2)
-    level_x = spread(level, lane_sc[...], 3)
+    both = range(2)
+    S = kq_ref.shape[3] // 2
+    own = [slice(r * N, (r + 1) * N) for r in both]
+    shifts = [shift_sc[r] for r in both]
+    depth = [depth_sc[own[r], 0:1] for r in both]
+    kq_taps = [row_of(kqw_ref[k], g) for k in range(4)]
+    kq = []
+    for r in both:
+        rows = jnp.where(
+            g == 0, kq_ref[slots[r], :, 0, :].astype(f32), kq_ref[slots[r], :, 1, :].astype(f32)
+        )
+        cache = [row_of(kqcache_ref[r, k], g) for k in range(3)]
+        kq.append(conv(rows.astype(bf16), cache, kq_taps, shifts[r], depth[r]))
+    key_b = [x[:, :S].astype(bf16) for x in kq]
+    query_b = [x[:, S:].astype(bf16) for x in kq]
+    levels = level_sc[g]
+    steps = size_sc[g]
+    stack, decay_m = [], []
+    for r in both:
+        level = levels[own[r]]
+        level_m = jnp.sum(
+            jnp.where(iota((N, H), 0) == size_s[r] - 1, level, 0.0), axis=0, keepdims=True
+        )
+        last_decay = jnp.exp(jnp.where(last_sc[own[r], :] > 0.5, level_m - level, -1e30))
+        decay_m.append(jnp.exp(level_m))
+        stack += [steps[own[r]], jnp.exp(level), last_decay]
+    wide = spread(jnp.concatenate(stack + [skip_sc[g]], axis=0), chan_sc[...], 2)
+    level_all = spread(levels, lane_sc[...], 3)
     diag = lax.rem(iota((N, H * N), 1), N) == iota((N, H * N), 0)
-    level_row = jnp.sum(jnp.where(diag, level_x, 0.0), axis=0, keepdims=True)
-    anc4 = anc_sc[own, :] > 0.5
-    key4 = jnp.concatenate([key] * 4, axis=0)
-    affinity4 = lax.dot_general(query, key4, NT, precision=highest, preferred_element_type=f32)
+    level_x = [level_all[own[r]] for r in both]
+    level_row = [jnp.sum(jnp.where(diag, x, 0.0), axis=0, keepdims=True) for x in level_x]
+    anc4 = [anc_sc[own[r], :] > 0.5 for r in both]
+    affinity4 = [
+        lax.dot_general(
+            x[:, S:], jnp.concatenate([x[:, :S]] * 4, axis=0), NT, precision=highest,
+            preferred_element_type=f32,
+        )
+        for x in kq
+    ]
     block_mask = iota((4 * N, 4 * PD), 0) // N == iota((4 * N, 4 * PD), 1) // PD
 
-    pieces = []
+    pieces = [[], []]
     for q in range(H // 4):
         cs = slice(q * 4 * PD, (q + 1) * 4 * PD)
         ls = slice(q * 4 * N, (q + 1) * 4 * N)
         taps = vw_ref[:, cs].astype(f32)
-        values = conv(
-            val_ref[slot, :, cs],
-            [row_of(vcache_ref[k, :, cs], r) for k in range(3)],
-            [taps[k:k + 1] for k in range(4)],
-        )
-        gap = level_x[:, ls] - level_row[:, ls]
-        weights = affinity4 * jnp.exp(jnp.where(anc4, gap, -1e30))
-        stepped = values * wide[0:N, cs]
-        four = jnp.concatenate([stepped] * 4, axis=0)
-        four = jnp.where(block_mask, four, 0.0).astype(bf16)
-        inner = dot(weights.astype(bf16), four)
-        state = state_ref[0, 4 * q:4 * q + 4].reshape(4 * PD, S)
-        carried = lax.dot_general(query_b, state.astype(bf16), NT, preferred_element_type=f32)
-        result = inner + carried * wide[N:2 * N, cs] + wide[3 * N:3 * N + 1, cs] * values
-        pieces.append(result * silu(gate_ref[slot, :, cs].astype(f32)))
-        scaled = (stepped * wide[2 * N:3 * N, cs]).astype(bf16)
-        update = lax.dot_general(scaled, key_b, TN, preferred_element_type=f32)
-        for k in range(4):
-            h = 4 * q + k
-            final_ref[0, h] = (
-                jnp.broadcast_to(decay_m[:, h:h + 1], (PD, S)) * state_ref[0, h]
-                + update[k * PD:(k + 1) * PD]
-            )
-    square = sum(jnp.sum(p * p, axis=1, keepdims=True) for p in pieces)
-    inverse = lax.rsqrt(square / C + norm_epsilon)
-    live = iota((N, 1), 0) < size_s[r]
-    a_row, a_col = iota((half, half), 0), iota((half, half), 1)
-    over = jnp.where(r == 1, jnp.maximum(size_s[0] - half, 0), 0)
-    pack = jnp.where(a_row == a_col + over, 1.0, 0.0).astype(bf16)
-    for q, piece in enumerate(pieces):
+        taps = [taps[k:k + 1] for k in range(4)]
+        skip = wide[6 * N:6 * N + 1, cs]
+        for r in both:
+            base = 3 * N * r
+            cache = [row_of(vcache_ref[k, :, cs], r) for k in range(3)]
+            values = conv(val_ref[slots[r], :, cs], cache, taps, shifts[r], depth[r])
+            gap = level_x[r][:, ls] - level_row[r][:, ls]
+            weights = affinity4[r] * jnp.exp(jnp.where(anc4[r], gap, -1e30))
+            stepped = values * wide[base:base + N, cs]
+            four = jnp.concatenate([stepped] * 4, axis=0)
+            four = jnp.where(block_mask, four, 0.0).astype(bf16)
+            inner = dot(weights.astype(bf16), four)
+            state = state_ref[r, 4 * q:4 * q + 4].reshape(4 * PD, S)
+            carried = lax.dot_general(query_b[r], state.astype(bf16), NT, preferred_element_type=f32)
+            result = inner + carried * wide[base + N:base + 2 * N, cs] + skip * values
+            pieces[r].append(result * silu(gate_ref[slots[r], :, cs].astype(f32)))
+            scaled = (stepped * wide[base + 2 * N:base + 3 * N, cs]).astype(bf16)
+            update = lax.dot_general(scaled, key_b[r], TN, preferred_element_type=f32)
+            for k in range(4):
+                h = 4 * q + k
+                final_ref[r, h] = (
+                    jnp.broadcast_to(decay_m[r][:, h:h + 1], (PD, S)) * state_ref[r, h]
+                    + update[k * PD:(k + 1) * PD]
+                )
+    inverse, live, pack = [], [], []
+    for r in both:
+        square = sum(jnp.sum(p * p, axis=1, keepdims=True) for p in pieces[r])
+        inverse.append(lax.rsqrt(square / C + norm_epsilon))
+        live.append(iota((N, 1), 0) < size_s[r])
+        over = jnp.maximum(size_s[0] - half, 0) * r
+        pack.append(
+            jnp.where(iota((half, half), 0) == iota((half, half), 1) + over, 1.0, 0.0).astype(bf16)
+        )
+    for q in range(H // 4):
         cs = slice(q * 4 * PD, (q + 1) * 4 * PD)
-        normed = piece * inverse * gain_ref[cs].astype(f32).reshape(1, -1)
-        hidden = jnp.where(live, normed, 0.0).astype(bf16)
-        hid_ref[0, pl.ds(pl.multiple_of(r * half, half), half), cs] = hidden[:half]
-        tail = dot(pack, hidden[half:])
-
-        @pl.when(r == 0)
-        def _():
-            hid_ref[0, N:, cs] = tail.astype(bf16)
-
-        @pl.when(r == 1)
-        def _():
-            hid_ref[0, N:, cs] = (hid_ref[0, N:, cs].astype(f32) + tail).astype(bf16)
+        gain = gain_ref[cs].astype(f32).reshape(1, -1)
+        tail = None
+        for r in both:
+            hidden = jnp.where(live[r], pieces[r][q] * inverse[r] * gain, 0.0).astype(bf16)
+            hid_ref[0, r * half:(r + 1) * half, cs] = hidden[:half]
+            term = dot(pack[r], hidden[half:])
+            tail = term if tail is None else tail + term
+        hid_ref[0, N:, cs] = tail.astype(bf16)
 
 
 def comm_kernel(
@@ -445,13 +455,13 @@
     packed_rows = N + N // 2
     caches = value_cache.transpose(1, 0, 2)
     smem = pl.BlockSpec(memory_space=pltpu.SMEM)
-    whole = lambda x: pl.BlockSpec(x.shape, lambda g, r: (0,) * x.ndim)
-    by_group = lambda x, n: pl.BlockSpec(x.shape[:-1] + (n,), lambda g, r: (0,) * (x.ndim - 1) + (g,))
+    whole = lambda x: pl.BlockSpec(x.shape, lambda g: (0,) * x.ndim)
+    by_group = lambda x, n: pl.BlockSpec(x.shape[:-1] + (n,), lambda g: (0,) * (x.ndim - 1) + (g,))
     bias, rate, skip = (x.reshape(1, -1) for x in (step_bias, log_rate, skip_gain))
-    state_spec = pl.BlockSpec((1, H, PD, S), lambda g, r: (r, g, 0, 0))
+    state_spec = pl.BlockSpec((Q, H, PD, S), lambda g: (0, g, 0, 0))
     packed, unpack, final_state = pl.pallas_call(
         ssm_kernel,
-        grid=(G, Q),
+        grid=(G,),
         out_shape=(
             jax.ShapeDtypeStruct((G, packed_rows, CG), bf16),
             jax.ShapeDtypeStruct((N, N // 2), bf16),
@@ -461,11 +471,11 @@
             smem, smem, smem,
             by_group(value_stream, CG), by_group(gate_stream, CG), whole(key_query_stream), whole(step_stream),
             by_group(caches, CG), whole(key_query_cache), by_group(value_conv, CG),
-            whole(key_query_conv), whole(bias), whole(rate), whole(skip), pl.BlockSpec((CG,), lambda g, r: (g,)), state_spec,
+            whole(key_query_conv), whole(bias), whole(rate), whole(skip), pl.BlockSpec((CG,), lambda g: (g,)), state_spec,
         ],
         out_specs=(
-            pl.BlockSpec((1, packed_rows, CG), lambda g, r: (g, 0, 0)),
-            pl.BlockSpec((N, N // 2), lambda g, r: (0, 0)),
+            pl.BlockSpec((1, packed_rows, CG), lambda g: (g, 0, 0)),
+            pl.BlockSpec((N, N // 2), lambda g: (0, 0)),
             state_spec,
         ),
         scratch_shapes=[

time: 73.2 us -> 69.9 us (0.955)
  Pallas kernels: 70.5 us -> 67.2 us
    pallas_call x1, Pallas kernels: 17.2 us -> 13.8 us  [local(): pl.pallas_call(ssm_kernel, grid=(G,), out_shape=(jax.ShapeDtypeStruct((G,...]
where the time goes in v3:
time: 69.9 us; the launch traced here: 69.7 us
  Pallas kernels  67.2 us (96%)
  local copies, waits for them, and re-layouts  1.87 us (3%)
    pallas_call x1, Pallas kernels, local(): pl.pallas_call(functools.partial(comm_kernel, R), out_shape=jax.ShapeDtyp...  53.3 us
    pallas_call x1, Pallas kernels, local(): pl.pallas_call(ssm_kernel, grid=(G,), out_shape=(jax.ShapeDtypeStruct((G,...  13.8 us
    unnamed x1, local copies, waits for them, and re-layouts  1.87 us

profile of v3, /device:TPU:0, one launch (start us, length us, event | category | flops | bytes accessed | tf_op | source)
XLA Modules:
  0.0 69.7 jit_solution(6828550812861748091)
XLA Ops:
  0.6 13.8 %ssm.1 = (bf16[2,48,2048]{2,1,0:T(8,128)(2,1)}, bf16[32,16]{1,0:T(8,128)(2,1)}, f32[2,64,64,256]{3,2,1,0:T(8,128)}) custom-call(s32[2]{0:T(128)} %slot_s.1, s32[2]{0:T(128)} %size_s.1, s32[2,32]{1,0:T(2,128)} %parent_s.1, bf16[2,32,4096]{2,1,0:T(8,128)(2,1)} %val_ref.1, bf16[2,32,4096]{2,1,0:T(8,128)(2,1)} %gate_ref.1, bf16[2,32,2,512]{3,2,1,0:T(2,128)(2,1)} %kq_ref.1, ...), custom_call_target="tpu_custom_call" | custom-call | tf_op jit(solution)/shard_map/ssm/pallas_call | solution.py:462
  14.5 53.3 %project.1 = bf16[2,16,8192]{2,1,0:T(8,128)(2,1)} custom-call(bf16[2,48,2048]{2,1,0:T(8,128)(2,1)} %get-tuple-element.5.packed, bf16[32,16]{1,0:T(8,128)(2,1)} %get-tuple-element.6.unpack, bf16[4096,1024]{1,0:T(8,128)(2,1)} %w_any.1), custom_call_target="tpu_custom_call" | custom-call | tf_op jit(solution)/shard_map/project/pallas_call | solution.py:501
  67.8 1.9 %copy.20 = bf16[2,16,8192]{2,1,0:T(8,128)(2,1)} copy(bf16[2,16,8192]{2,1,0:T(8,128)(2,1)} %project.1) | data formatting | bytes 1048576

commit v4 on v3

--- a/solution.py
+++ b/solution.py
@@ -272,9 +272,9 @@
     depth = gath.shape[3]
 
     def multiply(slot, first, second):
-        @pl.loop(0, cols // 256)
+        @pl.loop(0, cols // 512)
         def _(t):
-            at = pl.ds(pl.multiple_of(t * 256, 256), 256)
+            at = pl.ds(pl.multiple_of(t * 512, 512), 512)
             part[slot, :, at] = dot(first[...], wbuf[:depth, at]) + dot(second[...], wbuf[depth:, at])
         by_core(lambda mine, theirs: exchange(slot, *theirs).start())
 

time: 69.9 us -> 68.9 us (0.986)
  Pallas kernels: 67.2 us -> 66.2 us
    pallas_call x1, Pallas kernels: 53.3 us -> 52.4 us  [local(): pl.pallas_call(functools.partial(comm_kernel, R), out_shape=jax.ShapeDtyp...]
where the time goes in v4:
time: 68.9 us; the launch traced here: 68.7 us
  Pallas kernels  66.2 us (96%)
  local copies, waits for them, and re-layouts  1.87 us (3%)
    pallas_call x1, Pallas kernels, local(): pl.pallas_call(functools.partial(comm_kernel, R), out_shape=jax.ShapeDtyp...  52.4 us
    pallas_call x1, Pallas kernels, local(): pl.pallas_call(ssm_kernel, grid=(G,), out_shape=(jax.ShapeDtypeStruct((G,...  13.8 us
    unnamed x1, local copies, waits for them, and re-layouts  1.87 us

profile of v4, /device:TPU:0, one launch (start us, length us, event | category | flops | bytes accessed | tf_op | source)
XLA Modules:
  0.0 68.7 jit_solution(13744133576784356662)
XLA Ops:
  0.6 13.8 %ssm.1 = (bf16[2,48,2048]{2,1,0:T(8,128)(2,1)}, bf16[32,16]{1,0:T(8,128)(2,1)}, f32[2,64,64,256]{3,2,1,0:T(8,128)}) custom-call(s32[2]{0:T(128)} %slot_s.1, s32[2]{0:T(128)} %size_s.1, s32[2,32]{1,0:T(2,128)} %parent_s.1, bf16[2,32,4096]{2,1,0:T(8,128)(2,1)} %val_ref.1, bf16[2,32,4096]{2,1,0:T(8,128)(2,1)} %gate_ref.1, bf16[2,32,2,512]{3,2,1,0:T(2,128)(2,1)} %kq_ref.1, ...), custom_call_target="tpu_custom_call" | custom-call | tf_op jit(solution)/shard_map/ssm/pallas_call | solution.py:462
  14.5 52.4 %project.1 = bf16[2,16,8192]{2,1,0:T(8,128)(2,1)} custom-call(bf16[2,48,2048]{2,1,0:T(8,128)(2,1)} %get-tuple-element.5.packed, bf16[32,16]{1,0:T(8,128)(2,1)} %get-tuple-element.6.unpack, bf16[4096,1024]{1,0:T(8,128)(2,1)} %w_any.1), custom_call_target="tpu_custom_call" | custom-call | tf_op jit(solution)/shard_map/project/pallas_call | solution.py:501
  66.9 1.9 %copy.20 = bf16[2,16,8192]{2,1,0:T(8,128)(2,1)} copy(bf16[2,16,8192]{2,1,0:T(8,128)(2,1)} %project.1) | data formatting | bytes 1048576
